TPU v7x, 256 devices: a whole 4x4x8 slice. The times are simulated.
256 devices in a mesh: row: 16 (over y, z_hi), col: 16 (over z_lo, x, core).
Axes of the slice: x: 4, y: 4, z: 8 (z_hi: 4, z_lo: 2; z = z_hi * 2 + z_lo), core: 2. Of those that a mesh axis runs over, the one named last changes fastest.
Arguments:
- block_values: float32 [16, 16, 64, 128, 128], P('row', 'col')
- block_slot: int32 [16, 16, 64], P('row', 'col'), may hold values from 0 to 1023, as said below
- block_count: int32 [16, 16], P('row', 'col'), may hold values from 16 to 64, as said below
- probes: float32 [65536, 128], P(('row', 'col'))
Outputs:
- embedding: float32 [65536, 128], P(('row', 'col'))
- velocity: float32 [65536, 128], P(('row', 'col'))
Inputs may be any that keep to these rules, and one draw needn't show every extreme that they name: `block_slot`: the 64 positions of one group tile are distinct; a position s stands for local block row s // 32 and local block column s % 32; of the positions with equal (s // 32) // 2 and (s % 32) // 2, at most 1 are among them, and some such group holds 1. The slots k < block_count[r, c] are in use, the others are not part of W; some tile uses all 64 slots.
All inputs are finite; a program needn't handle non-finite values. Where the computation divides by a largest or mean magnitude, that divisor is 1e-20 or more.
Results may differ from a plain program's by a relative error of at most 0.00024.
Values sent between devices are 32-bit elements; how exact they have to be, the bound alone decides.
No kernel may reach another device: no remote copies, remote signals or barrier semaphores. Data moves between devices by JAX's collectives and lax.ppermute only.
A program may use at most 192 MiB of HBM per device.

v0:
```python
import jax
import jax.numpy as jnp
from jax import lax
from jax.sharding import PartitionSpec as P

BLK = 128
ITERS = 3


def local(block_values, block_slot, block_count, probes):
    row_devices = lax.axis_size("row")
    column_devices = lax.axis_size("col")
    piece_rows = probes.shape[0]
    per_piece = piece_rows // BLK
    tile_rows = per_piece * column_devices
    tile_columns = per_piece * row_devices
    total_docs = piece_rows * row_devices * column_devices
    slots = block_slot.reshape(-1)
    stored = slots.shape[0]
    local_row = slots // tile_columns
    local_column = slots % tile_columns
    in_use = jnp.arange(stored, dtype=jnp.int32) < block_count.reshape(())
    masked = jnp.where(in_use[:, None, None], block_values.reshape(stored, BLK, BLK), 0.0)
    row_onehot = (jnp.arange(tile_rows, dtype=jnp.int32)[:, None] == local_row[None, :]).astype(
        jnp.float32
    )
    row_weight = jnp.dot(
        row_onehot, jnp.sum(masked, axis=2), precision=lax.Precision.HIGHEST
    ).reshape(tile_rows * BLK)
    column_onehot = (
        jnp.arange(tile_columns, dtype=jnp.int32)[:, None] == local_column[None, :]
    ).astype(jnp.float32)
    column_weight = jnp.dot(
        column_onehot, jnp.sum(masked, axis=1), precision=lax.Precision.HIGHEST
    ).reshape(tile_columns * BLK)
    current = probes
    earlier = probes
    for iteration in range(ITERS):
        width = current.shape[1]
        column_group = lax.all_gather(current, "row", axis=0, tiled=True).reshape(
            tile_columns, BLK, width
        )
        forward = jnp.einsum(
            "kab,kbp->kap",
            masked,
            jnp.take(column_group, local_column, axis=0),
            precision=lax.Precision.HIGHEST,
        )
        row_partial = jnp.einsum(
            "rk,kap->rap", row_onehot, forward, precision=lax.Precision.HIGHEST
        ).reshape(tile_rows * BLK, width)
        row_total = lax.psum_scatter(row_partial, "col", scatter_dimension=0, tiled=True)
        row_degree = lax.psum_scatter(row_weight, "col", scatter_dimension=0, tiled=True)
        row_group = lax.all_gather(current, "col", axis=0, tiled=True).reshape(
            tile_rows, BLK, width
        )
        backward = jnp.einsum(
            "kba,kbp->kap",
            masked,
            jnp.take(row_group, local_row, axis=0),
            precision=lax.Precision.HIGHEST,
        )
        column_partial = jnp.einsum(
            "ck,kap->cap", column_onehot, backward, precision=lax.Precision.HIGHEST
        ).reshape(tile_columns * BLK, width)
        column_total = lax.psum_scatter(column_partial, "row", scatter_dimension=0, tiled=True)
        column_degree = lax.psum_scatter(column_weight, "row", scatter_dimension=0, tiled=True)
        averaged = (row_total + column_total) / (row_degree + column_degree)[:, None]
        mean_abs = lax.psum(jnp.sum(jnp.abs(averaged), axis=0), ("row", "col")) / total_docs
        earlier = current
        current = averaged / mean_abs
    return (current, current - earlier)


def solution(mesh):
    in_specs = (
        P("row", "col", None, None, None),
        P("row", "col", None),
        P("row", "col"),
        P(("row", "col"), None),
    )
    out_specs = (P(("row", "col"), None), P(("row", "col"), None))
    return jax.shard_map(local, mesh=mesh, in_specs=in_specs, out_specs=out_specs, check_vma=False)
```

profile of v0, /device:TPU:24, one launch (start us, length us, event | category | flops | bytes accessed | tf_op | source)
XLA Modules:
  0.0 1009.0 jit_solution(5408173570652164270)
XLA Ops:
  10.0 62.3 %all-gather.7.cloned.1.call-done = f32[4096,128]{1,0:T(8,128)} async-done(((f32[256,128]{1,0:T(8,128)}), f32[4096,128]{1,0:T(8,128)}) %all-gather.7.cloned.1.call-update) | async-done | bytes 2097168 | tf_op jit(solution)/shard_map/all_gather | solution.py:40
  72.3 4.3 gather_fusion
  76.7 7.1 fusion.22
  90.7 18.4 %all-gather.9.cloned.1.call-done = f32[4096,128]{1,0:T(8,128)} async-done(((f32[256,128]{1,0:T(8,128)}), f32[4096,128]{1,0:T(8,128)}) %all-gather.9.cloned.1.call-update) | async-done | bytes 2097168 | tf_op jit(solution)/shard_map/all_gather | solution.py:54
  109.1 4.3 gather_fusion.1
  113.4 9.6 fusion.20
  135.8 54.7 %all-reduce = f32[4096]{0:T(1024)S(1)} all-reduce(f32[4096]{0:T(1024)S(1)} %convolution_bitcast_fusion.1), channel_id=4, replica_groups=mesh['row'=16,'col'=16] {'col'}, use_global_device_ids=true, to_apply=%region_3.5.clone | all-reduce | flops 4096 | bytes 32768
  190.6 76.0 %all-reduce.1 = f32[4096]{0:T(1024)S(1)} all-reduce(f32[4096]{0:T(1024)S(1)} %convolution_bitcast_fusion), channel_id=5, replica_groups=mesh['row'=16,'col'=16] {'row'}, use_global_device_ids=true, to_apply=%region_5.7.clone | all-reduce | flops 4096 | bytes 32768
  267.8 78.2 %psum.21 = f32[128]{0:T(128)S(1)} all-reduce(f32[128]{0:T(128)S(1)} %get-tuple-element.11), channel_id=1, replica_groups=mesh['row'=16,'col'=16] {'row','col'}, use_global_device_ids=true, to_apply=%region_7.9 | all-reduce | flops 128 | bytes 1024 | tf_op jit(solution)/shard_map/psum | solution.py:69
  347.5 31.5 %all-gather.13.cloned.1.call-done = f32[4096,128]{1,0:T(8,128)} async-done(((f32[256,128]{1,0:T(8,128)}), f32[4096,128]{1,0:T(8,128)}) %all-gather.13.cloned.1.call-update) | async-done | bytes 2097168 | tf_op jit(solution)/shard_map/all_gather | solution.py:54
  378.9 4.3 gather_fusion.3
  383.3 9.6 fusion.16
  399.7 41.4 %all-gather.11.cloned.1.call-done = f32[4096,128]{1,0:T(8,128)} async-done(((f32[256,128]{1,0:T(8,128)}), f32[4096,128]{1,0:T(8,128)}) %all-gather.11.cloned.1.call-update) | async-done | bytes 2097168 | tf_op jit(solution)/shard_map/all_gather | solution.py:40
  445.4 7.1 fusion.18
  459.2 71.4 %reduce-scatter.13.cloned.1.call-done = f32[256,128]{1,0:T(8,128)} async-done(((f32[4096,128]{1,0:T(8,128)}), f32[256,128]{1,0:T(8,128)}) %reduce-scatter.13.cloned.1.call-update) | async-done | bytes 131088 | tf_op jit(solution)/shard_map/reduce_scatter | solution.py:66
  530.6 67.2 %reduce-scatter.11.cloned.1.call-done = f32[256,128]{1,0:T(8,128)} async-done(((f32[4096,128]{1,0:T(8,128)}), f32[256,128]{1,0:T(8,128)}) %reduce-scatter.11.cloned.1.call-update) | async-done | bytes 131088 | tf_op jit(solution)/shard_map/reduce_scatter | solution.py:52
  598.9 73.9 %psum.22 = f32[128]{0:T(128)S(1)} all-reduce(f32[128]{0:T(128)S(1)} %get-tuple-element.9), channel_id=1, replica_groups=mesh['row'=16,'col'=16] {'row','col'}, use_global_device_ids=true, to_apply=%region_11.13 | all-reduce | flops 128 | bytes 1024 | tf_op jit(solution)/shard_map/psum | solution.py:69
  674.5 33.4 %all-gather.17.cloned.1.call-done = f32[4096,128]{1,0:T(8,128)} async-done(((f32[256,128]{1,0:T(8,128)}), f32[4096,128]{1,0:T(8,128)}) %all-gather.17.cloned.1.call-update) | async-done | bytes 2097168 | tf_op jit(solution)/shard_map/all_gather | solution.py:54
  712.2 9.6 fusion.12
  728.8 41.0 %all-gather.15.cloned.1.call-done = f32[4096,128]{1,0:T(8,128)} async-done(((f32[256,128]{1,0:T(8,128)}), f32[4096,128]{1,0:T(8,128)}) %all-gather.15.cloned.1.call-update) | async-done | bytes 2097168 | tf_op jit(solution)/shard_map/all_gather | solution.py:40
  774.1 7.1 fusion.14
  787.8 70.9 %reduce-scatter.17.cloned.1.call-done = f32[256,128]{1,0:T(8,128)} async-done(((f32[4096,128]{1,0:T(8,128)}), f32[256,128]{1,0:T(8,128)}) %reduce-scatter.17.cloned.1.call-update) | async-done | bytes 131088 | tf_op jit(solution)/shard_map/reduce_scatter | solution.py:66
  858.7 67.2 %reduce-scatter.15.cloned.1.call-done = f32[256,128]{1,0:T(8,128)} async-done(((f32[4096,128]{1,0:T(8,128)}), f32[256,128]{1,0:T(8,128)}) %reduce-scatter.15.cloned.1.call-update) | async-done | bytes 131088 | tf_op jit(solution)/shard_map/reduce_scatter | solution.py:52
  927.0 73.9 %psum.23 = f32[128]{0:T(128)S(1)} all-reduce(f32[128]{0:T(128)S(1)} %get-tuple-element.7), channel_id=1, replica_groups=mesh['row'=16,'col'=16] {'row','col'}, use_global_device_ids=true, to_apply=%region_15.17 | all-reduce | flops 128 | bytes 1024 | tf_op jit(solution)/shard_map/psum | solution.py:69
  (65 shorter events, 67.9 us)
Async XLA Ops:
  7.2 65.2 %all-gather.7.cloned.1.call-start = ((), (), s32[]{:S(2)}) async-start(), calls=%async_computation.6 | async-start | bytes 2228224 | tf_op jit(solution)/shard_map/all_gather | solution.py:40
  7.9 101.2 %all-gather.9.cloned.1.call-start = ((), (), s32[]{:S(2)}) async-start(), calls=%async_computation.8 | async-start | bytes 2228224 | tf_op jit(solution)/shard_map/all_gather | solution.py:54
  8.6 258.1 %reduce-scatter.7.cloned.1.call-start = ((), (), s32[]{:S(2)}) async-start(), calls=%async_computation.7 | async-start | bytes 2228224 | tf_op jit(solution)/shard_map/reduce_scatter | solution.py:52
  90.4 176.3 %reduce-scatter.9.cloned.1.call-start = ((), (), s32[]{:S(2)}) async-start(), calls=%async_computation.9 | async-start | bytes 2228224 | tf_op jit(solution)/shard_map/reduce_scatter | solution.py:66
  127.0 2.7 copy-start.1
  127.0 3.9 copy-start
  129.7 249.3 %all-gather.13.cloned.1.call-start = ((), (), s32[]{:S(2)}) async-start(), calls=%async_computation.12 | async-start | bytes 2228224 | tf_op jit(solution)/shard_map/all_gather | solution.py:54
  346.9 94.2 %all-gather.11.cloned.1.call-start = ((), (), s32[]{:S(2)}) async-start(), calls=%async_computation.10 | async-start | bytes 2228224 | tf_op jit(solution)/shard_map/all_gather | solution.py:40
  347.4 183.2 %reduce-scatter.13.cloned.1.call-start = ((), (), s32[]{:S(2)}) async-start(), calls=%async_computation.13 | async-start | bytes 2228224 | tf_op jit(solution)/shard_map/reduce_scatter | solution.py:66
  399.5 198.3 %reduce-scatter.11.cloned.1.call-start = ((), (), s32[]{:S(2)}) async-start(), calls=%async_computation.11 | async-start | bytes 2228224 | tf_op jit(solution)/shard_map/reduce_scatter | solution.py:52
  459.2 248.7 %all-gather.17.cloned.1.call-start = ((), (), s32[]{:S(2)}) async-start(), calls=%async_computation.16 | async-start | bytes 2228224 | tf_op jit(solution)/shard_map/all_gather | solution.py:54
  673.6 96.1 %all-gather.15.cloned.1.call-start = ((), (), s32[]{:S(2)}) async-start(), calls=%async_computation.14 | async-start | bytes 2228224 | tf_op jit(solution)/shard_map/all_gather | solution.py:40
  674.2 184.5 %reduce-scatter.17.cloned.1.call-start = ((), (), s32[]{:S(2)}) async-start(), calls=%async_computation.17 | async-start | bytes 2228224 | tf_op jit(solution)/shard_map/reduce_scatter | solution.py:66
  728.5 197.4 %reduce-scatter.15.cloned.1.call-start = ((), (), s32[]{:S(2)}) async-start(), calls=%async_computation.15 | async-start | bytes 2228224 | tf_op jit(solution)/shard_map/reduce_scatter | solution.py:52
Sparse Core Ops, SparseCore 0:
  10.4 61.8 all-gather.6
  74.2 34.8 all-gather.8
  111.6 65.7 reduce-scatter.6
  180.8 85.4 reduce-scatter.8
  347.0 31.9 all-gather.12
  382.1 58.9 all-gather.10
  445.1 85.5 reduce-scatter.12
  533.2 64.6 reduce-scatter.10
  673.7 34.1 all-gather.16
  710.8 58.9 all-gather.14
  773.3 85.3 reduce-scatter.16
  861.3 64.5 reduce-scatter.14
where the time goes:
time: 1020 us; the launch traced here: 1010 us
  waiting for transfers between devices  507 us (50%)
  blocking collectives  357 us (35%)
  matrix products  74.6 us (7%)
  local copies, waits for them, and re-layouts  42.6 us (4%)
  between operations  16.8 us (2%)
    psum x3, blocking collectives, local(): lax.psum(jnp.sum(jnp.abs(averaged), axis=0), ('row', 'col')) / total_docs  226 us
    all_gather x3, waiting for transfers between devices, local(): lax.all_gather(current, 'row', axis=0, tiled=True)  145 us
    reduce_scatter x3, waiting for transfers between devices, local(): lax.psum_scatter(column_partial, 'row', scatter_dimension=0, tiled=True)  142 us
    reduce_scatter x3, waiting for transfers between devices, local(): lax.psum_scatter(row_partial, 'col', scatter_dimension=0, tiled=True)  134 us
    unnamed x2, blocking collectives  131 us
    all_gather x3, waiting for transfers between devices, local(): lax.all_gather(current, 'col', axis=0, tiled=True)  83.3 us
    dot_general x3, matrix products, local(): jnp.einsum('kba,kbp->kap', masked, jnp.take(row_group, local_row, axis=0)...  28.7 us
    dot_general x3, matrix products, local(): jnp.einsum('kab,kbp->kap', masked, jnp.take(column_group, local_column, a...  21.3 us
  transfers between devices with their start and end apart: 12, of which 10 were waited for; matrix products, arithmetic and copies ran while one was open for 12% of the time, Pallas kernels for 0%

commit v1 on v0

v1 whole, which is shorter than its diff:
```python
import functools

import jax
import jax.numpy as jnp
from jax import lax
from jax.experimental import pallas as pl
from jax.experimental.pallas import tpu as pltpu
from jax.sharding import PartitionSpec as P

BLK = 128
ITERS = 3
VMEM_LIMIT = 40 * 1024 * 1024

ROW_ORDER = [4 * y + z for y, z in (
    (0, 0), (0, 1), (1, 0), (1, 1), (3, 0), (3, 1), (2, 0), (2, 1),
    (0, 3), (0, 2), (3, 3), (3, 2), (1, 3), (1, 2), (2, 3), (2, 2))]
COL_ORDER = [8 * l + 2 * x + c for c in (0, 1) for l, x in (
    (0, 0), (0, 1), (0, 3), (0, 2), (1, 0), (1, 3), (1, 1), (1, 2))]


def swap(x, axis, m):
    return lax.ppermute(x, axis, [(i, i ^ m) for i in range(16)])


def row_swap(x, y=0, z=0):
    return swap(x, "row", 4 * y + z)


def col_swap(x, l=0, x_=0, c=0):
    return swap(x, "col", 8 * l + 2 * x_ + c)


def cat(*parts):
    return jnp.concatenate(parts, axis=0)


def gather_row(x):
    r = row_swap(x, z=1)
    a = cat(x, r)
    b = row_swap(a, z=3)
    a1 = cat(a, row_swap(a, y=1))
    b1 = cat(b, row_swap(b, y=3))
    a2 = row_swap(a1, y=3)
    b2 = row_swap(b1, y=1)
    return [a1, a2, b1, b2]


def gather_col(x):
    b = col_swap(x, l=1)
    a1 = cat(x, col_swap(x, x_=1))
    b1 = cat(b, col_swap(b, x_=3))
    a2 = col_swap(a1, x_=3)
    b2 = col_swap(b1, x_=1)
    return [a1, a2, b1, b2] + [col_swap(p, c=1) for p in (a1, a2, b1, b2)]


def scatter_row(a_keep, a_send, b_keep, b_send):
    a_got = row_swap(a_send, y=3)
    b_got = row_swap(b_send, y=1)
    h = a_keep.shape[0] // 2
    a_got2 = row_swap(a_keep[h:] + a_got[h:], y=1)
    b_got2 = row_swap(b_keep[h:] + b_got[h:], y=3)
    b2 = b_keep[:h] + b_got[:h] + b_got2
    got3 = row_swap(b2, z=3)
    a2 = a_keep[:h] + a_got[:h] + a_got2
    q = h // 2
    got4 = row_swap(a2[q:] + got3[q:], z=1)
    return a2[:q] + got3[:q] + got4


def scatter_col(keep, send):
    got = col_swap(send, c=1)
    q = keep.shape[0] // 4
    part = [keep[i * q:(i + 1) * q] + got[i * q:(i + 1) * q] for i in range(4)]
    a_got = col_swap(part[1], x_=3)
    b_got = col_swap(part[3], x_=1)
    h = q // 2
    a_got2 = col_swap(part[0][h:] + a_got[h:], x_=1)
    b_got2 = col_swap(part[2][h:] + b_got[h:], x_=3)
    got2 = col_swap(part[2][:h] + b_got[:h] + b_got2, l=1)
    return part[0][:h] + a_got[:h] + a_got2 + got2


def global_sum(s):
    for kw in (dict(c=1), dict(x_=1), dict(x_=3), dict(l=1)):
        s = s + col_swap(s, **kw)
    for kw in (dict(z=1), dict(z=3), dict(y=1), dict(y=3)):
        s = s + row_swap(s, **kw)
    return s


def prepare_kernel(row_ref, col_ref, count_ref, w_ref, wh, wl, th, tl, drow, dcol):
    step = pl.program_id(0)

    @pl.when(step == 0)
    def _():
        drow[...] = jnp.zeros_like(drow)
        dcol[...] = jnp.zeros_like(dcol)

    per = w_ref.shape[0]
    for j in range(per):
        k = step * per + j
        w = jnp.where(k < count_ref[0], w_ref[j], 0.0)
        t = w.T
        hi = w.astype(jnp.bfloat16)
        wh[j] = hi
        wl[j] = (w - hi.astype(jnp.float32)).astype(jnp.bfloat16)
        hi = t.astype(jnp.bfloat16)
        th[j] = hi
        tl[j] = (t - hi.astype(jnp.float32)).astype(jnp.bfloat16)
        first = lax.broadcasted_iota(jnp.int32, (8, BLK), 0) == 0
        r, c = row_ref[k], col_ref[k]
        drow[r] += jnp.where(first, jnp.sum(t, axis=0, keepdims=True), 0.0)
        dcol[c] += jnp.where(first, jnp.sum(w, axis=0, keepdims=True), 0.0)


def prepare(values, row_pos, col_pos, count):
    n = values.shape[0]
    per = 8
    nrow, ncol = 32, 32
    blk = pl.BlockSpec((per, BLK, BLK), lambda i, *_: (i, 0, 0))
    deg = pl.BlockSpec((nrow, 8, BLK), lambda i, *_: (0, 0, 0))
    half = jax.ShapeDtypeStruct((n, BLK, BLK), jnp.bfloat16)
    return pl.pallas_call(
        prepare_kernel,
        grid_spec=pltpu.PrefetchScalarGridSpec(
            num_scalar_prefetch=3, grid=(n // per,), in_specs=[blk], out_specs=[blk] * 4 + [deg] * 2
        ),
        out_shape=[half] * 4
        + [jax.ShapeDtypeStruct((nrow, 8, BLK), jnp.float32), jax.ShapeDtypeStruct((ncol, 8, BLK), jnp.float32)],
        compiler_params=pltpu.CompilerParams(vmem_limit_bytes=VMEM_LIMIT),
        name="prepare",
    )(row_pos, col_pos, count, values)


def product_kernel(n_in, n_out, with_deg, src_ref, dst_ref, *refs):
    refs = list(refs)
    wh, wl, inv = refs[:3]
    xs = refs[3:3 + n_in]
    rest = refs[3 + n_in:]
    if with_deg:
        deg, rest = rest[0], rest[1:]
    outs, (xh, xl, acc) = rest[:n_out], rest[n_out:]
    scale = inv[...]
    at = 0
    for x in xs:
        for b in range(x.shape[0] // BLK):
            v = x[b * BLK:(b + 1) * BLK, :] / scale
            hi = v.astype(jnp.bfloat16)
            xh[at] = hi
            xl[at] = (v - hi.astype(jnp.float32)).astype(jnp.bfloat16)
            at += 1
    acc[...] = jnp.zeros_like(acc)
    group = 4

    @pl.loop(0, wh.shape[0] // group)
    def _(g):
        prods = []
        for j in range(group):
            k = g * group + j
            s = src_ref[k]
            a, b, c, d = wh[k], wl[k], xh[s], xl[s]
            p = jnp.dot(a, c, preferred_element_type=jnp.float32)
            p += jnp.dot(b, c, preferred_element_type=jnp.float32)
            p += jnp.dot(a, d, preferred_element_type=jnp.float32)
            prods.append(p)
        for j in range(group):
            d = dst_ref[g * group + j]
            acc[d] += prods[j]

    at = 0
    for o in outs:
        for b in range(o.shape[0]):
            o[b, :BLK, :] = acc[at]
            if with_deg:
                o[b, BLK:, :] = deg[at]
            at += 1


def product(src, dst, wh, wl, mean, xs, sizes, deg=None):
    rows = BLK + (8 if deg is not None else 0)
    smem = pl.BlockSpec(memory_space=pltpu.SMEM)
    vmem = pl.BlockSpec(memory_space=pltpu.VMEM)
    args = [wh, wl, mean, *xs] + ([deg] if deg is not None else [])
    n = wh.shape[0]
    return pl.pallas_call(
        functools.partial(product_kernel, len(xs), len(sizes), deg is not None),
        in_specs=[smem, smem] + [vmem] * len(args),
        out_specs=[vmem] * len(sizes),
        out_shape=[jax.ShapeDtypeStruct((s, rows, BLK), jnp.float32) for s in sizes],
        scratch_shapes=[
            pltpu.VMEM((32, BLK, BLK), jnp.bfloat16),
            pltpu.VMEM((32, BLK, BLK), jnp.bfloat16),
            pltpu.VMEM((32, BLK, BLK), jnp.float32),
        ],
        compiler_params=pltpu.CompilerParams(vmem_limit_bytes=VMEM_LIMIT),
        cost_estimate=pl.CostEstimate(flops=6 * n * BLK**3, bytes_accessed=12 * 2**20, transcendentals=0),
        name="product",
    )(src, dst, *args)


def finish_kernel(r_ref, c_ref, y_ref, d_ref, s_ref):
    total = jnp.zeros((8, BLK), jnp.float32)
    for b in range(2):
        t = r_ref[b] + c_ref[b]
        d = jnp.broadcast_to(t[BLK:BLK + 1, :], (BLK, BLK)).T
        y = t[:BLK] / d
        y_ref[b * BLK:(b + 1) * BLK, :] = y
        d_ref[b * BLK:(b + 1) * BLK, :] = d
        total += jnp.sum(jnp.abs(y).reshape(BLK // 8, 8, BLK), axis=0)
    s_ref[...] = jnp.broadcast_to(jnp.sum(total, axis=0, keepdims=True), (8, BLK))


def finish_first(r, c):
    vmem = pl.BlockSpec(memory_space=pltpu.VMEM)
    big = jax.ShapeDtypeStruct((2 * BLK, BLK), jnp.float32)
    return pl.pallas_call(
        finish_kernel,
        in_specs=[vmem, vmem],
        out_specs=[vmem] * 3,
        out_shape=[big, big, jax.ShapeDtypeStruct((8, BLK), jnp.float32)],
        name="finish",
    )(r, c)


def position(order, index):
    order_pos = [order.index(m) for m in range(16)]
    out = jnp.zeros_like(index)
    for m in range(16):
        out = out + jnp.where(index == m, order_pos[m], 0)
    return out


def local(block_values, block_slot, block_count, probes):
    total_docs = probes.shape[0] * lax.axis_size("row") * lax.axis_size("col")
    slots = block_slot.reshape(-1)
    stored = slots.shape[0]
    local_row, local_col = slots // 32, slots % 32
    row_pos = 2 * position(COL_ORDER, (local_row // 2) ^ lax.axis_index("col")) + local_row % 2
    col_pos = 2 * position(ROW_ORDER, (local_col // 2) ^ lax.axis_index("row")) + local_col % 2
    wh, wl, th, tl, drow, dcol = prepare(
        block_values.reshape(stored, BLK, BLK), row_pos, col_pos, block_count.reshape(1)
    )
    mean = jnp.ones((1, BLK), jnp.float32)
    y = probes
    means = []
    ys = []
    for t in range(ITERS):
        col_parts = gather_col(y)
        row_parts = gather_row(y)
        back = product(row_pos, col_pos, th, tl, mean, col_parts, [8] * 4, dcol if t == 0 else None)
        col_total = scatter_row(*back)
        fwd = product(col_pos, row_pos, wh, wl, mean, row_parts, [16, 16], drow if t == 0 else None)
        row_total = scatter_col(*fwd)
        if t == 0:
            y, deg, part = finish_first(row_total, col_total)
        else:
            y = (row_total + col_total).reshape(2 * BLK, BLK) / deg
            part = jnp.broadcast_to(jnp.sum(jnp.abs(y), axis=0, keepdims=True), (8, BLK))
        mean = global_sum(part)[:1] / total_docs
        means.append(mean)
        ys.append(y)
    current = ys[-1] / means[-1]
    return current, current - ys[-2] / means[-2]


def solution(mesh):
    in_specs = (
        P("row", "col", None, None, None),
        P("row", "col", None),
        P("row", "col"),
        P(("row", "col"), None),
    )
    out_specs = (P(("row", "col"), None), P(("row", "col"), None))
    return jax.shard_map(local, mesh=mesh, in_specs=in_specs, out_specs=out_specs, check_vma=False)
```

time: 1020 us -> 407 us (0.40)
  blocking collectives: 357 us -> 0 us
  waiting for transfers between devices: 507 us -> 214 us
  starting transfers between devices: 1.33 us -> 134 us
  matrix products: 74.6 us -> 0 us
  Pallas kernels: 0 us -> 39.8 us
  local copies, waits for them, and re-layouts: 42.6 us -> 8.06 us
  between operations: 16.8 us -> 2.29 us
    reduce_scatter x6 -> x0, waiting for transfers between devices: 277 us -> none  [the longest x3 142 us: local(): lax.psum_scatter(column_partial, 'row', scatter_dimension=0, tiled=True)]
    all_gather x6 -> x0, waiting for transfers between devices: 228 us -> none  [the longest x3 145 us: local(): lax.all_gather(current, 'row', axis=0, tiled=True)]
    psum x3 -> x0, blocking collectives: 226 us -> none  [local(): lax.psum(jnp.sum(jnp.abs(averaged), axis=0), ('row', 'col')) / total_docs]
    ppermute x0 -> x105, waiting for transfers between devices: none -> 214 us  [swap(): return lax.ppermute(x, axis, [(i, i ^ m) for i in range(16)])]
    ppermute x0 -> x105, starting transfers between devices: none -> 134 us  [swap(): return lax.ppermute(x, axis, [(i, i ^ m) for i in range(16)])]
    unnamed x2 -> x0, blocking collectives: 131 us -> none
    dot_general x14 -> x0, matrix products: 74.6 us -> none  [the longest x3 28.7 us: local(): jnp.einsum('kba,kbp->kap', masked, jnp.take(row_group, local_row, axis=0)...]
    pallas_call x0 -> x8, Pallas kernels: none -> 39.8 us  [the longest x6 35.6 us: product(): pl.pallas_call(functools.partial(product_kernel, len(xs), len(sizes), deg...]
  transfers between devices with their start and end apart: 12 -> 105, of which waited for: 10 -> 58; matrix products, arithmetic and copies ran while one was open for 12% -> 2% of each run, Pallas kernels for 0% -> 9%
where the time goes in v1:
time: 407 us; the launch traced here: 402 us
  waiting for transfers between devices  214 us (53%)
  starting transfers between devices  134 us (33%)
  Pallas kernels  39.8 us (10%)
  local copies, waits for them, and re-layouts  8.06 us (2%)
  other arithmetic  4.41 us (1%)
    ppermute x105, waiting for transfers between devices, swap(): return lax.ppermute(x, axis, [(i, i ^ m) for i in range(16)])  214 us
    ppermute x105, starting transfers between devices, swap(): return lax.ppermute(x, axis, [(i, i ^ m) for i in range(16)])  134 us
    pallas_call x6, Pallas kernels, product(): pl.pallas_call(functools.partial(product_kernel, len(xs), len(sizes), deg...  35.6 us
  transfers between devices with their start and end apart: 105, of which 58 were waited for; matrix products, arithmetic and copies ran while one was open for 2% of the time, Pallas kernels for 9%

profile of v1, /device:TPU:24, one launch (start us, length us, event | category | flops | bytes accessed | tf_op | source)
XLA Modules:
  0.0 402.5 jit_solution(6403818252502329234)
XLA Ops:
  19.3 6.1 %collective-permute-done.3 = f32[512,128]{1,0:T(8,128)S(1)} collective-permute-done((f32[512,128]{1,0:T(8,128)S(1)}, f32[512,128]{1,0:T(8,128)S(1)}, u32[]{:S(2)}, u32[]{:S(2)}) %collective-permute-start.3) | collective-permute-done | bytes 262176 | tf_op jit(solution)/shard_map/ppermute | solution.py:22
  30.8 5.1 %collective-permute-done.4 = f32[512,128]{1,0:T(8,128)S(1)} collective-permute-done((f32[512,128]{1,0:T(8,128)S(1)}, f32[512,128]{1,0:T(8,128)S(1)}, u32[]{:S(2)}, u32[]{:S(2)}) %collective-permute-start.4) | collective-permute-done | bytes 262176 | tf_op jit(solution)/shard_map/ppermute | solution.py:22
  42.7 7.6 %product.7 = (f32[8,136,128]{2,1,0:T(8,128)S(1)}, f32[8,136,128]{2,1,0:T(8,128)S(1)}, f32[8,136,128]{2,1,0:T(8,128)S(1)}, f32[8,136,128]{2,1,0:T(8,128)S(1)}) custom-call(s32[64]{0:T(128)S(1)} %get-tuple-element.85.row_ref.dst_ref.src_ref, s32[64]{0:T(128)S(1)} %get-tuple-element.84.col_ref.src_ref.dst_ref, ...), custom_call_target="tpu_custom_call" | custom-call | flops 805306368 | bytes 12582912 | tf_op jit(solution)/shard_map/product/pallas_call | solution.py:186
  52.3 6.1 %product.6 = (f32[16,136,128]{2,1,0:T(8,128)S(1)}, f32[16,136,128]{2,1,0:T(8,128)S(1)}) custom-call(s32[64]{0:T(128)S(1)} %get-tuple-element.84.col_ref.src_ref.dst_ref, s32[64]{0:T(128)S(1)} %get-tuple-element.85.row_ref.dst_ref.src_ref, bf16[64,128,128]{2,1,0:T(8,128)(2,1)S(1)} %get-tuple-element.29.refs_0_, ...), custom_call_target="tpu_custom_call" | custom-call | flops 805306368 | bytes 12582912 | tf_op jit(solution)/shard_map/product/pallas_call | solution.py:186
  58.9 6.6 %collective-permute-done.23 = f32[8,136,128]{2,1,0:T(8,128)S(1)} collective-permute-done((f32[8,136,128]{2,1,0:T(8,128)S(1)}, f32[8,136,128]{2,1,0:T(8,128)S(1)}, u32[]{:S(2)}, u32[]{:S(2)}) %collective-permute-start.23) | collective-permute-done | bytes 557088 | tf_op jit(solution)/shard_map/ppermute | solution.py:22
  66.0 9.6 %collective-permute-done.21 = f32[8,136,128]{2,1,0:T(8,128)S(1)} collective-permute-done((f32[8,136,128]{2,1,0:T(8,128)S(1)}, f32[8,136,128]{2,1,0:T(8,128)S(1)}, u32[]{:S(2)}, u32[]{:S(2)}) %collective-permute-start.21) | collective-permute-done | bytes 557088 | tf_op jit(solution)/shard_map/ppermute | solution.py:22
  75.7 5.2 %collective-permute-done.24 = f32[4,136,128]{2,1,0:T(8,128)S(1)} collective-permute-done((f32[4,136,128]{2,1,0:T(8,128)S(1)}, f32[4,136,128]{2,1,0:T(8,128)S(1)}, u32[]{:S(2)}, u32[]{:S(2)}) %collective-permute-start.24) | collective-permute-done | bytes 278560 | tf_op jit(solution)/shard_map/ppermute | solution.py:22
  81.0 4.7 %collective-permute-start.25 = (f32[4,136,128]{2,1,0:T(8,128)S(1)}, f32[4,136,128]{2,1,0:T(8,128)S(1)}, u32[]{:S(2)}, u32[]{:S(2)}) collective-permute-start(f32[4,136,128]{2,1,0:T(8,128)S(1)} %fusion), channel_id=1, source_target_pairs={{0,48},{16,32},{32,16},{48,0},{64,112},{80,96},{96,80},{112,64},{1... | collective-permute-start | bytes 835592 | tf_op jit(solution)/shard_map/ppermute | solution.py:22
  89.5 6.0 %collective-permute-done.25 = f32[4,136,128]{2,1,0:T(8,128)S(1)} collective-permute-done((f32[4,136,128]{2,1,0:T(8,128)S(1)}, f32[4,136,128]{2,1,0:T(8,128)S(1)}, u32[]{:S(2)}, u32[]{:S(2)}) %collective-permute-start.25) | collective-permute-done | bytes 278560 | tf_op jit(solution)/shard_map/ppermute | solution.py:22
  150.9 8.6 %collective-permute-start.36 = (f32[512,128]{1,0:T(8,128)S(1)}, f32[512,128]{1,0:T(8,128)S(1)}, u32[]{:S(2)}, u32[]{:S(2)}) collective-permute-start(f32[512,128]{1,0:T(8,128)S(1)} %get-tuple-element.74), channel_id=1, source_target_pairs={{0,64},{16,80},{32,96},{48,112},{64,0},{80,16},{96,32},{112,48},{1... | collective-permute-start | bytes 786440 | tf_op jit(solution)/shard_map/ppermute | solution.py:22
  168.8 7.0 %collective-permute-done.39 = f32[512,128]{1,0:T(8,128)S(1)} collective-permute-done((f32[512,128]{1,0:T(8,128)S(1)}, f32[512,128]{1,0:T(8,128)S(1)}, u32[]{:S(2)}, u32[]{:S(2)}) %collective-permute-start.39) | collective-permute-done | bytes 262176 | tf_op jit(solution)/shard_map/ppermute | solution.py:22
  182.6 5.5 %product.9 = (f32[8,128,128]{2,1,0:T(8,128)S(1)}, f32[8,128,128]{2,1,0:T(8,128)S(1)}, f32[8,128,128]{2,1,0:T(8,128)S(1)}, f32[8,128,128]{2,1,0:T(8,128)S(1)}) custom-call(s32[64]{0:T(128)S(1)} %get-tuple-element.85.row_ref.dst_ref.src_ref, s32[64]{0:T(128)S(1)} %get-tuple-element.84.col_ref.src_ref.dst_ref, bf16[64,128,128]{2,1,0:T(8,128)(2,1)S(1)} %copy-done.3, ...), custom_call_target="tpu_custom_call" | custom-call | flops 805306368 | bytes 12582912 | tf_op jit(solution)/shard_map/product/pallas_call | solution.py:186
  192.7 5.5 %product.8 = (f32[16,128,128]{2,1,0:T(8,128)S(1)}, f32[16,128,128]{2,1,0:T(8,128)S(1)}) custom-call(s32[64]{0:T(128)S(1)} %get-tuple-element.84.col_ref.src_ref.dst_ref, s32[64]{0:T(128)S(1)} %get-tuple-element.85.row_ref.dst_ref.src_ref, bf16[64,128,128]{2,1,0:T(8,128)(2,1)S(1)} %get-tuple-element.29.refs_0_, bf16[64,128,128]{2,1,0:T(8,128)(2,1)S(1)} %copy-done.1, ...), custom_call_target="tpu_custom_call" | custom-call | flops 805306368 | bytes 12582912 | tf_op jit(solution)/shard_map/product/pallas_call | solution.py:186
  203.8 10.6 %collective-permute-done.56 = f32[8,128,128]{2,1,0:T(8,128)S(1)} collective-permute-done((f32[8,128,128]{2,1,0:T(8,128)S(1)}, f32[8,128,128]{2,1,0:T(8,128)S(1)}, u32[]{:S(2)}, u32[]{:S(2)}) %collective-permute-start.56) | collective-permute-done | bytes 524320 | tf_op jit(solution)/shard_map/ppermute | solution.py:22
  214.5 5.0 %collective-permute-done.59 = f32[4,128,128]{2,1,0:T(8,128)S(1)} collective-permute-done((f32[4,128,128]{2,1,0:T(8,128)S(1)}, f32[4,128,128]{2,1,0:T(8,128)S(1)}, u32[]{:S(2)}, u32[]{:S(2)}) %collective-permute-start.59) | collective-permute-done | bytes 262176 | tf_op jit(solution)/shard_map/ppermute | solution.py:22
  225.7 7.4 %collective-permute-done.60 = f32[4,128,128]{2,1,0:T(8,128)S(1)} collective-permute-done((f32[4,128,128]{2,1,0:T(8,128)S(1)}, f32[4,128,128]{2,1,0:T(8,128)S(1)}, u32[]{:S(2)}, u32[]{:S(2)}) %collective-permute-start.60) | collective-permute-done | bytes 262176 | tf_op jit(solution)/shard_map/ppermute | solution.py:22
  288.4 7.1 %collective-permute-done.74 = f32[512,128]{1,0:T(8,128)S(1)} collective-permute-done((f32[512,128]{1,0:T(8,128)S(1)}, f32[512,128]{1,0:T(8,128)S(1)}, u32[]{:S(2)}, u32[]{:S(2)}) %collective-permute-start.74) | collective-permute-done | bytes 262176 | tf_op jit(solution)/shard_map/ppermute | solution.py:22
  300.7 5.5 %product.11 = (f32[8,128,128]{2,1,0:T(8,128)S(1)}, f32[8,128,128]{2,1,0:T(8,128)S(1)}, f32[8,128,128]{2,1,0:T(8,128)S(1)}, f32[8,128,128]{2,1,0:T(8,128)S(1)}) custom-call(s32[64]{0:T(128)S(1)} %get-tuple-element.85.row_ref.dst_ref.src_ref, s32[64]{0:T(128)S(1)} %get-tuple-element.84.col_ref.src_ref.dst_ref, bf16[64,128,128]{2,1,0:T(8,128)(2,1)S(1)} %copy-done.3, ...), custom_call_target="tpu_custom_call" | custom-call | flops 805306368 | bytes 12582912 | tf_op jit(solution)/shard_map/product/pallas_call | solution.py:186
  313.2 5.5 %product.10 = (f32[16,128,128]{2,1,0:T(8,128)S(1)}, f32[16,128,128]{2,1,0:T(8,128)S(1)}) custom-call(s32[64]{0:T(128)S(1)} %get-tuple-element.84.col_ref.src_ref.dst_ref, s32[64]{0:T(128)S(1)} %get-tuple-element.85.row_ref.dst_ref.src_ref, bf16[64,128,128]{2,1,0:T(8,128)(2,1)S(1)} %get-tuple-element.29.refs_0_, bf16[64,128,128]{2,1,0:T(8,128)(2,1)S(1)} %copy-done.1, ...), custom_call_target="tpu_custom_call" | custom-call | flops 805306368 | bytes 12582912 | tf_op jit(solution)/shard_map/product/pallas_call | solution.py:186
  323.5 11.3 %collective-permute-done.91 = f32[8,128,128]{2,1,0:T(8,128)S(1)} collective-permute-done((f32[8,128,128]{2,1,0:T(8,128)S(1)}, f32[8,128,128]{2,1,0:T(8,128)S(1)}, u32[]{:S(2)}, u32[]{:S(2)}) %collective-permute-start.91) | collective-permute-done | bytes 524320 | tf_op jit(solution)/shard_map/ppermute | solution.py:22
  334.9 5.0 %collective-permute-done.94 = f32[4,128,128]{2,1,0:T(8,128)S(1)} collective-permute-done((f32[4,128,128]{2,1,0:T(8,128)S(1)}, f32[4,128,128]{2,1,0:T(8,128)S(1)}, u32[]{:S(2)}, u32[]{:S(2)}) %collective-permute-start.94) | collective-permute-done | bytes 262176 | tf_op jit(solution)/shard_map/ppermute | solution.py:22
  344.1 9.5 %collective-permute-done.95 = f32[4,128,128]{2,1,0:T(8,128)S(1)} collective-permute-done((f32[4,128,128]{2,1,0:T(8,128)S(1)}, f32[4,128,128]{2,1,0:T(8,128)S(1)}, u32[]{:S(2)}, u32[]{:S(2)}) %collective-permute-start.95) | collective-permute-done | bytes 262176 | tf_op jit(solution)/shard_map/ppermute | solution.py:22
  359.1 5.0 %collective-permute-done.80 = f32[2,128,128]{2,1,0:T(8,128)S(1)} collective-permute-done((f32[2,128,128]{2,1,0:T(8,128)S(1)}, f32[2,128,128]{2,1,0:T(8,128)S(1)}, u32[]{:S(2)}, u32[]{:S(2)}) %collective-permute-start.80) | collective-permute-done | bytes 131104 | tf_op jit(solution)/shard_map/ppermute | solution.py:22
  364.3 4.9 %collective-permute-done.81 = f32[2,128,128]{2,1,0:T(8,128)S(1)} collective-permute-done((f32[2,128,128]{2,1,0:T(8,128)S(1)}, f32[2,128,128]{2,1,0:T(8,128)S(1)}, u32[]{:S(2)}, u32[]{:S(2)}) %collective-permute-start.81) | collective-permute-done | bytes 131104 | tf_op jit(solution)/shard_map/ppermute | solution.py:22
  (305 shorter events, 239.9 us)
Async XLA Ops:
  18.2 17.8 %collective-permute-start.13 = (f32[512,128]{1,0:T(8,128)S(1)}, f32[512,128]{1,0:T(8,128)}, u32[]{:S(2)}, u32[]{:S(2)}) collective-permute-start(f32[512,128]{1,0:T(8,128)S(1)} %constant_dynamic-update-slice_fusion.7.refs_3_), channel_id=1, source_target_pairs={{0,6},{1,7},{2,4},{3,5},{4,2},{5,3},{6,0},{7,1},{8,14},{9,15},{10,... | collective-permute-start | bytes 786440 | tf_op jit(solution)/shard_map/ppermute | solution.py:22
  18.6 17.5 %collective-permute-start.17 = (f32[512,128]{1,0:T(8,128)S(1)}, f32[512,128]{1,0:T(8,128)S(1)}, u32[]{:S(2)}, u32[]{:S(2)}) collective-permute-start(f32[512,128]{1,0:T(8,128)S(1)} %constant_dynamic-update-slice_fusion.7.refs_3_), channel_id=1, source_target_pairs={{0,1},{1,0},{2,3},{3,2},{4,5},{5,4},{6,7},{7,6},{8,9},{9,8},{10,11... | collective-permute-start | bytes 786440 | tf_op jit(solution)/shard_map/ppermute | solution.py:22
  27.6 24.7 %collective-permute-start.2 = (f32[1024,128]{1,0:T(8,128)S(1)}, f32[1024,128]{1,0:T(8,128)}, u32[]{:S(2)}, u32[]{:S(2)}) collective-permute-start(f32[1024,128]{1,0:T(8,128)S(1)} %constant_dynamic-update-slice_fusion.2.refs_3_), channel_id=1, source_target_pairs={{0,192},{16,208},{32,224},{48,240},{64,128},{80,144},{96,160},{112... | collective-permute-start | bytes 1572872 | tf_op jit(solution)/shard_map/ppermute | solution.py:22
  35.8 16.4 %collective-permute-start.5 = (f32[1024,128]{1,0:T(8,128)S(1)}, f32[1024,128]{1,0:T(8,128)}, u32[]{:S(2)}, u32[]{:S(2)}) collective-permute-start(f32[1024,128]{1,0:T(8,128)S(1)} %constant_dynamic-update-slice_fusion.5.refs_5_), channel_id=1, source_target_pairs={{0,64},{16,80},{32,96},{48,112},{64,0},{80,16},{96,32},{112,48},{1... | collective-permute-start | bytes 1572872 | tf_op jit(solution)/shard_map/ppermute | solution.py:22
  58.4 27.3 %collective-permute-start.6 = (f32[16,136,128]{2,1,0:T(8,128)S(1)}, f32[16,136,128]{2,1,0:T(8,128)S(1)}, u32[]{:S(2)}, u32[]{:S(2)}) collective-permute-start(f32[16,136,128]{2,1,0:T(8,128)S(1)} %get-tuple-element.33), channel_id=1, source_target_pairs={{0,1},{1,0},{2,3},{3,2},{4,5},{5,4},{6,7},{7,6},{8,9},{9,8},{10,11... | collective-permute-start | bytes 3342344 | tf_op jit(solution)/shard_map/ppermute | solution.py:22
  58.7 16.9 %collective-permute-start.21 = (f32[8,136,128]{2,1,0:T(8,128)S(1)}, f32[8,136,128]{2,1,0:T(8,128)S(1)}, u32[]{:S(2)}, u32[]{:S(2)}) collective-permute-start(f32[8,136,128]{2,1,0:T(8,128)S(1)} %get-tuple-element.38), channel_id=1, source_target_pairs={{0,192},{16,208},{32,224},{48,240},{64,128},{80,144},{96,160},{112... | collective-permute-start | bytes 1671176 | tf_op jit(solution)/shard_map/ppermute | solution.py:22
  114.7 47.7 %collective-permute-start.47 = (f32[256,128]{1,0:T(8,128)}, f32[256,128]{1,0:T(8,128)S(1)}, u32[]{:S(2)}, u32[]{:S(2)}) collective-permute-start(f32[256,128]{1,0:T(8,128)} %get-tuple-element.42), channel_id=1, source_target_pairs={{0,2},{1,3},{2,0},{3,1},{4,6},{5,7},{6,4},{7,5},{8,10},{9,11},{10,... | collective-permute-start | bytes 393224 | tf_op jit(solution)/shard_map/ppermute | solution.py:22
  114.8 44.8 %collective-permute-start.49 = (f32[256,128]{1,0:T(8,128)}, f32[256,128]{1,0:T(8,128)S(1)}, u32[]{:S(2)}, u32[]{:S(2)}) collective-permute-start(f32[256,128]{1,0:T(8,128)} %get-tuple-element.42), channel_id=1, source_target_pairs={{0,8},{1,9},{2,10},{3,11},{4,12},{5,13},{6,14},{7,15},{8,0},{9,1},... | collective-permute-start | bytes 393224 | tf_op jit(solution)/shard_map/ppermute | solution.py:22
  121.3 44.5 %collective-permute-start.38 = (f32[512,128]{1,0:T(8,128)S(1)}, f32[512,128]{1,0:T(8,128)S(1)}, u32[]{:S(2)}, u32[]{:S(2)}) collective-permute-start(f32[512,128]{1,0:T(8,128)S(1)} %get-tuple-element.74), channel_id=1, source_target_pairs={{0,48},{16,32},{32,16},{48,0},{64,112},{80,96},{96,80},{112,64},{1... | collective-permute-start | bytes 786440 | tf_op jit(solution)/shard_map/ppermute | solution.py:22
  150.4 28.1 %collective-permute-start.34 = (f32[8,128]{1,0:T(8,128)S(1)}, f32[8,128]{1,0:T(8,128)S(1)}, u32[]{:S(2)}, u32[]{:S(2)}) collective-permute-start(f32[8,128]{1,0:T(8,128)S(1)} %add.426), channel_id=1, source_target_pairs={{0,192},{16,208},{32,224},{48,240},{64,128},{80,144},{96,160},{112... | collective-permute-start | bytes 12296 | tf_op jit(solution)/shard_map/ppermute | solution.py:22
  150.9 17.7 %collective-permute-start.36 = (f32[512,128]{1,0:T(8,128)S(1)}, f32[512,128]{1,0:T(8,128)S(1)}, u32[]{:S(2)}, u32[]{:S(2)}) collective-permute-start(f32[512,128]{1,0:T(8,128)S(1)} %get-tuple-element.74), channel_id=1, source_target_pairs={{0,64},{16,80},{32,96},{48,112},{64,0},{80,16},{96,32},{112,48},{1... | collective-permute-start | bytes 786440 | tf_op jit(solution)/shard_map/ppermute | solution.py:22
  162.4 16.3 %collective-permute-start.48 = (f32[512,128]{1,0:T(8,128)S(1)}, f32[512,128]{1,0:T(8,128)S(1)}, u32[]{:S(2)}, u32[]{:S(2)}) collective-permute-start(f32[512,128]{1,0:T(8,128)S(1)} %constant_dynamic-update-slice_fusion.18.refs_3_), channel_id=1, source_target_pairs={{0,6},{1,7},{2,4},{3,5},{4,2},{5,3},{6,0},{7,1},{8,14},{9,15},{10,... | collective-permute-start | bytes 786440 | tf_op jit(solution)/shard_map/ppermute | solution.py:22
  198.2 24.5 %collective-permute-start.41 = (f32[16,128,128]{2,1,0:T(8,128)S(1)}, f32[16,128,128]{2,1,0:T(8,128)S(1)}, u32[]{:S(2)}, u32[]{:S(2)}) collective-permute-start(f32[16,128,128]{2,1,0:T(8,128)S(1)} %get-tuple-element.44), channel_id=1, source_target_pairs={{0,1},{1,0},{2,3},{3,2},{4,5},{5,4},{6,7},{7,6},{8,9},{9,8},{10,11... | collective-permute-start | bytes 3145736 | tf_op jit(solution)/shard_map/ppermute | solution.py:22
  198.3 16.0 %collective-permute-start.56 = (f32[8,128,128]{2,1,0:T(8,128)S(1)}, f32[8,128,128]{2,1,0:T(8,128)S(1)}, u32[]{:S(2)}, u32[]{:S(2)}) collective-permute-start(f32[8,128,128]{2,1,0:T(8,128)S(1)} %get-tuple-element.46), channel_id=1, source_target_pairs={{0,192},{16,208},{32,224},{48,240},{64,128},{80,144},{96,160},{112... | collective-permute-start | bytes 1572872 | tf_op jit(solution)/shard_map/ppermute | solution.py:22
  203.2 16.3 %collective-permute-start.59 = (f32[4,128,128]{2,1,0:T(8,128)S(1)}, f32[4,128,128]{2,1,0:T(8,128)S(1)}, u32[]{:S(2)}, u32[]{:S(2)}) collective-permute-start(f32[4,128,128]{2,1,0:T(8,128)S(1)} %slice_add_fusion.16), channel_id=1, source_target_pairs={{0,192},{16,208},{32,224},{48,240},{64,128},{80,144},{96,160},{112... | collective-permute-start | bytes 786440 | tf_op jit(solution)/shard_map/ppermute | solution.py:22
  223.0 17.3 %collective-permute-start.42 = (f32[4,128,128]{2,1,0:T(8,128)S(1)}, f32[4,128,128]{2,1,0:T(8,128)S(1)}, u32[]{:S(2)}, u32[]{:S(2)}) collective-permute-start(f32[4,128,128]{2,1,0:T(8,128)S(1)} %get-tuple-element.71), channel_id=1, source_target_pairs={{0,6},{1,7},{2,4},{3,5},{4,2},{5,3},{6,0},{7,1},{8,14},{9,15},{10,... | collective-permute-start | bytes 786440 | tf_op jit(solution)/shard_map/ppermute | solution.py:22
  249.9 16.8 %collective-permute-start.84 = (f32[256,128]{1,0:T(8,128)S(1)}, f32[256,128]{1,0:T(8,128)S(1)}, u32[]{:S(2)}, u32[]{:S(2)}) collective-permute-start(f32[256,128]{1,0:T(8,128)S(1)} %get-tuple-element.59), channel_id=1, source_target_pairs={{0,8},{1,9},{2,10},{3,11},{4,12},{5,13},{6,14},{7,15},{8,0},{9,1},... | collective-permute-start | bytes 393224 | tf_op jit(solution)/shard_map/ppermute | solution.py:22
  258.5 29.7 %collective-permute-start.71 = (f32[512,128]{1,0:T(8,128)S(1)}, f32[512,128]{1,0:T(8,128)S(1)}, u32[]{:S(2)}, u32[]{:S(2)}) collective-permute-start(f32[512,128]{1,0:T(8,128)S(1)} %get-tuple-element.72), channel_id=1, source_target_pairs={{0,64},{16,80},{32,96},{48,112},{64,0},{80,16},{96,32},{112,48},{1... | collective-permute-start | bytes 786440 | tf_op jit(solution)/shard_map/ppermute | solution.py:22
  258.6 26.9 %collective-permute-start.73 = (f32[512,128]{1,0:T(8,128)S(1)}, f32[512,128]{1,0:T(8,128)S(1)}, u32[]{:S(2)}, u32[]{:S(2)}) collective-permute-start(f32[512,128]{1,0:T(8,128)S(1)} %get-tuple-element.72), channel_id=1, source_target_pairs={{0,48},{16,32},{32,16},{48,0},{64,112},{80,96},{96,80},{112,64},{1... | collective-permute-start | bytes 786440 | tf_op jit(solution)/shard_map/ppermute | solution.py:22
  266.7 18.7 %collective-permute-start.85 = (f32[256,128]{1,0:T(8,128)S(1)}, f32[256,128]{1,0:T(8,128)S(1)}, u32[]{:S(2)}, u32[]{:S(2)}) collective-permute-start(f32[256,128]{1,0:T(8,128)S(1)} %collective-permute-done.84), channel_id=1, source_target_pairs={{0,6},{1,7},{2,4},{3,5},{4,2},{5,3},{6,0},{7,1},{8,14},{9,15},{10,... | collective-permute-start | bytes 393224 | tf_op jit(solution)/shard_map/ppermute | solution.py:22
  306.2 16.5 %collective-permute-start.93 = (f32[8,128,128]{2,1,0:T(8,128)S(1)}, f32[8,128,128]{2,1,0:T(8,128)S(1)}, u32[]{:S(2)}, u32[]{:S(2)}) collective-permute-start(f32[8,128,128]{2,1,0:T(8,128)S(1)} %get-tuple-element.55), channel_id=1, source_target_pairs={{0,64},{16,80},{32,96},{48,112},{64,0},{80,16},{96,32},{112,48},{1... | collective-permute-start | bytes 1572872 | tf_op jit(solution)/shard_map/ppermute | solution.py:22
  318.7 24.6 %collective-permute-start.76 = (f32[16,128,128]{2,1,0:T(8,128)S(1)}, f32[16,128,128]{2,1,0:T(8,128)S(1)}, u32[]{:S(2)}, u32[]{:S(2)}) collective-permute-start(f32[16,128,128]{2,1,0:T(8,128)S(1)} %get-tuple-element.51), channel_id=1, source_target_pairs={{0,1},{1,0},{2,3},{3,2},{4,5},{5,4},{6,7},{7,6},{8,9},{9,8},{10,11... | collective-permute-start | bytes 3145736 | tf_op jit(solution)/shard_map/ppermute | solution.py:22
  318.8 16.0 %collective-permute-start.91 = (f32[8,128,128]{2,1,0:T(8,128)S(1)}, f32[8,128,128]{2,1,0:T(8,128)S(1)}, u32[]{:S(2)}, u32[]{:S(2)}) collective-permute-start(f32[8,128,128]{2,1,0:T(8,128)S(1)} %get-tuple-element.53), channel_id=1, source_target_pairs={{0,192},{16,208},{32,224},{48,240},{64,128},{80,144},{96,160},{112... | collective-permute-start | bytes 1572872 | tf_op jit(solution)/shard_map/ppermute | solution.py:22
  322.8 17.2 %collective-permute-start.94 = (f32[4,128,128]{2,1,0:T(8,128)S(1)}, f32[4,128,128]{2,1,0:T(8,128)S(1)}, u32[]{:S(2)}, u32[]{:S(2)}) collective-permute-start(f32[4,128,128]{2,1,0:T(8,128)S(1)} %slice_add_fusion.8), channel_id=1, source_target_pairs={{0,192},{16,208},{32,224},{48,240},{64,128},{80,144},{96,160},{112... | collective-permute-start | bytes 786440 | tf_op jit(solution)/shard_map/ppermute | solution.py:22
  (92 other events, 851.4 us)
